TPU v7x, 32 devices: a whole 2x2x4 slice. The times are simulated.
32 devices in a mesh: arch: 2 (over core), dom: 16 (over z, y, x).
Axes of the slice: x: 2, y: 2, z: 4, core: 2. Of those that a mesh axis runs over, the one named last changes fastest.
Arguments:
- position: float32 [3, 131072], P(None, ('arch', 'dom')), may hold values from -6 to 6
- particle_mass: float32 [131072], P(('arch', 'dom')), may hold values from 0.5 to 2
- settling: float32 [131072], P(('arch', 'dom')), may hold values from 0.05 to 1
- walk_noise: float32 [3, 3, 131072], P(None, None, ('arch', 'dom')), may hold values from -6 to 6
- velocity: bfloat16 [4, 3, 32, 2048], P(None, None, ('arch', 'dom')), may hold values from -6 to 6
- diffusivity: bfloat16 [4, 32, 2048], P(None, ('arch', 'dom')), may hold values from 0.019897461 to 0.5
- block_tile: int32 [3, 32, 16], P(None, ('arch', 'dom')), may hold values from 0 to 31, as said below
- cell_index: int32 [3, 131072], P(None, ('arch', 'dom')), may hold values from 0 to 2047
- bed_cell: int32 [3, 131072], P(None, ('arch', 'dom')), may hold values from 0 to 511
- route_code: int32 [2, 32, 16], P(None, ('arch', 'dom')), may hold values from 0 to 15, each once within a row
Outputs:
- final_position: float32 [3, 131072], P(None, ('arch', 'dom'))
- final_mass: float32 [131072], P(('arch', 'dom'))
- bed_deposit: float32 [32, 512], P(('arch', 'dom'))
Inputs may be any that keep to these rules, and one draw needn't show every extreme that they name: `block_tile`: in every step each block's tile belongs to the group of the block's dom index d: (tile) % 16 equals d. Within each group, tiles held at lower arch indices are used by more blocks than those at higher ones.
All inputs are finite; a program needn't handle non-finite values.
Results may differ from a plain program's by a relative error of at most 0.0003.
Values may be sent and summed in bfloat16 or wider, within the bound.
A program may use at most 64 MiB of HBM per device.

v0:
```python
import functools
import math

import jax
import jax.numpy as jnp
from jax import lax
from jax.experimental import pallas as pl
from jax.experimental.pallas import tpu as pltpu
from jax.sharding import PartitionSpec as P

MESH = pl.DeviceIdType.MESH
BF16 = jnp.bfloat16
F32 = jnp.float32

BEDC = 512
LANES = 128
time_step = 0.5


def kernel(
    doms, archs, nblocks, width, steps, slabs, rows, scale,
    pos_hbm, mass_hbm, settle_hbm, noise_hbm, vel_hbm, diff_hbm, tile_hbm, cell_hbm, bed_hbm, route_hbm,
    pos_out, mass_out, bed_out,
    pos, mass, settle, noise, vel, diff, tile, cell, bed, route,
    spread_rows, table, inverse, decay, dep, delta,
    carried_send, carried_recv, pos_send, pos_recv,
    bed_part, bed_recv,
    in_sem, table_sem, carried_sem, pos_sem, bed_sem,
):
    me = lax.axis_index("dom")
    arch = lax.axis_index("arch")
    twin = lax.rem(arch + 1, archs)
    group = math.gcd(nblocks, 16)

    staged = [
        pltpu.make_async_copy(src, dst, in_sem.at[i])
        for i, (src, dst) in enumerate(
            [
                (vel_hbm, vel), (diff_hbm, diff), (tile_hbm, tile), (route_hbm, route), (mass_hbm, mass),
                (settle_hbm, settle), (bed_hbm, bed), (cell_hbm, cell), (pos_hbm, pos), (noise_hbm, noise),
            ]
        )
    ]
    for copy in staged[:2]:
        copy.start()

    barrier = pltpu.get_barrier_semaphore()

    def greet(p, _):
        pl.semaphore_signal(barrier, inc=1, device_id={"dom": lax.rem(me + p, doms)}, device_id_type=MESH)
        return 0

    lax.fori_loop(1, doms, greet, 0)
    pl.semaphore_signal(barrier, inc=1, device_id={"arch": twin}, device_id_type=MESH)

    for copy in staged[2:]:
        copy.start()

    def find_inverse(step):
        def invert(c, _):
            def probe(j, found):
                return jnp.where(route[step, 0, j] == c, j, found)

            inverse[step, c] = lax.fori_loop(0, nblocks, probe, jnp.int32(0), unroll=True if nblocks <= 16 else 16)
            return 0

        lax.fori_loop(0, nblocks, invert, 0, unroll=4)

    for copy in staged[:2]:
        copy.wait()
    for ch in range(4):
        raw = (vel[ch] if ch < 3 else diff[...]).astype(F32)
        for r in range(rows):
            spread_rows[ch, pl.ds(r, slabs, stride=rows), :] = raw[:, r * LANES : (r + 1) * LANES]
    for slab in range(slabs):
        for ch in range(4):
            table[arch, slab, ch] = spread_rows[ch, slab * rows : (slab + 1) * rows, :].astype(BF16)

    pl.semaphore_wait(barrier, doms - 1 + archs - 1)

    table_copy = pltpu.make_async_remote_copy(
        src_ref=table.at[arch], dst_ref=table.at[arch], send_sem=table_sem.at[0], recv_sem=table_sem.at[1],
        device_id={"arch": twin}, device_id_type=MESH,
    )
    table_copy.start()

    for copy in staged[2:7]:
        copy.wait()
    fade = jnp.exp(-time_step * settle[...])
    decay[...] = fade
    dep[...] = mass[...] * (1.0 - fade)
    mass[...] = mass[...] * fade
    find_inverse(0)

    def send(step, sbuf, rbuf, sem, p):
        pltpu.make_async_remote_copy(
            src_ref=sbuf[step].at[p], dst_ref=rbuf[step].at[me], send_sem=sem.at[step, 0], recv_sem=sem.at[step, 1],
            device_id={"dom": lax.rem(me + p, doms)}, device_id_type=MESH,
        ).start()

    def whole(step, sbuf, rbuf, sem):
        return pltpu.make_async_remote_copy(
            src_ref=sbuf[step].at[pl.ds(1, doms - 1)], dst_ref=rbuf[step].at[pl.ds(1, doms - 1)],
            send_sem=sem.at[step, 0], recv_sem=sem.at[step, 1],
            device_id={"dom": lax.rem(me + 1, doms)}, device_id_type=MESH,
        )

    def send_carried(step, source):
        def load(p):
            return source(inverse[step, lax.rem(me + p, doms)])

        m, e = load(0)
        carried_recv[step][me, 0:2, :] = m
        carried_recv[step][me, 2:4, :] = e

        def one(p, _):
            m, e = load(p)
            carried_send[step][p, 0:2, :] = m
            carried_send[step][p, 2:4, :] = e
            send(step, carried_send, carried_recv, carried_sem, p)
            return 0

        lax.fori_loop(1, doms, one, 0, unroll=5 if doms == 16 else 1)

    send_carried(0, lambda j: (mass[j], decay[j]))

    tall_ids = lax.broadcasted_iota(jnp.int32, (LANES, width), 0).astype(BF16)
    cell_rows = lax.broadcasted_iota(jnp.int32, (rows, width), 0)
    home_rows = lax.broadcasted_iota(jnp.int32, (8, width), 0)

    def low_hits(cells):
        low = jnp.broadcast_to(lax.bitwise_and(cells, LANES - 1), (16, width)).astype(BF16)
        low = jnp.broadcast_to(low[None], (LANES // 16, 16, width)).reshape(LANES, width)
        return jnp.where(low == tall_ids, jnp.ones((), BF16), jnp.zeros((), BF16))

    def high_bits(cells):
        return lax.shift_right_logical(cells, 7)

    def deposits(step, blocks):
        weights, hits = [], []
        for j in blocks:
            cells = bed[step : step + 1, pl.ds(pl.multiple_of(j * width, width), width)]
            local = lax.div(tile[step, 0, j], doms)
            home = local * (BEDC // LANES) + high_bits(cells)
            amount = jnp.concatenate([dep[j, 0:1, :], dep[j, 1:2, :]], axis=1)
            weight = jnp.where(home == home_rows, amount, 0.0)
            high = weight.astype(BF16)
            low = (weight - high.astype(F32)).astype(BF16)
            weights.append(jnp.concatenate([high, low], axis=0))
            hits.append(low_hits(cells))
        return lax.dot_general(
            jnp.concatenate(weights, axis=1), jnp.concatenate(hits, axis=1),
            (((1,), (1,)), ((), ())), preferred_element_type=F32,
        )

    def all_deposits(step, total):
        def some(k, total):
            return total + deposits(step, [k * group + i for i in range(group)])

        return lax.fori_loop(0, nblocks // group, some, total)

    channel_ids = lax.broadcasted_iota(jnp.int32, (16, 2 * 4 * rows), 1) // rows % 4
    out_ids = lax.broadcasted_iota(jnp.int32, (16, 2 * 4 * rows), 0)
    mix = jnp.where(
        out_ids < 8,
        jnp.where(channel_ids == out_ids, 0.5 * time_step, 0.0),
        jnp.where(channel_ids == 3, time_step, 0.0),
    ).astype(BF16)

    def walk(step, blocks):
        picked = []
        for j in blocks:
            cells = cell[step : step + 1, pl.ds(pl.multiple_of(j * width, width), width)]
            row_hit = jnp.where(high_bits(cells) == cell_rows, 1.0, 0.0).astype(BF16)
            local = lax.div(tile[step, 0, j], doms)
            both = jnp.concatenate(
                [table[local, slab].reshape(4 * rows, LANES) for slab in (step, step + 1)], axis=0
            )
            found = jnp.dot(both, low_hits(cells), preferred_element_type=F32).astype(BF16)
            found = found.reshape(8, rows, width) * row_hit[None]
            picked.append(found.reshape(8 * rows, width))
        mixed = jnp.dot(mix, jnp.concatenate(picked, axis=1), preferred_element_type=F32)
        moves = []
        for i, j in enumerate(blocks):
            part = mixed[:, i * width : (i + 1) * width]
            draw = noise[step, :, pl.ds(pl.multiple_of(j * width, width), width)]
            moves.append(part[0:3] + jnp.sqrt(part[8:11]) * draw)
        return moves

    third = (lax.broadcasted_iota(jnp.int32, (3, width), 0) == 2)

    total = jnp.zeros((16, LANES), F32)

    for copy in staged[7:]:
        copy.wait()
    table_copy.wait_recv()

    def first(k, _):
        blocks = [k * group + i for i in range(group)]
        moves = walk(0, blocks)
        values = []
        for j, move in zip(blocks, moves):
            speed = jnp.concatenate([settle[j, 0:1, :], settle[j, 1:2, :]], axis=1)
            sink = jnp.where(third, steps * time_step * speed, 0.0)
            here = pos[:, pl.ds(pl.multiple_of(j * width, width), width)]
            values.append(here - sink + move)
        for j, value in zip(blocks, values):
            delta[j] = value
        return 0

    lax.fori_loop(0, nblocks // group, first, 0)

    def send_places(step, source):
        def one(p, _):
            pos_send[step][p] = source(inverse[step, lax.rem(me + p, doms)])
            send(step, pos_send, pos_recv, pos_sem, p)
            return 0

        lax.fori_loop(1, doms, one, 0, unroll=5 if doms == 16 else 1)
        pos_recv[step][me] = source(inverse[step, me])

    send_places(0, lambda j: delta[j])

    for step in range(1, steps):
        if step + 1 < steps:
            find_inverse(step)
        def some(k, total, step=step):
            blocks = [k * group + i for i in range(group)]
            moves = walk(step, blocks)
            total = total + deposits(step - 1, blocks)
            for j, move in zip(blocks, moves):
                delta[j] = move
            return total

        def forward(step=step):
            whole(step - 1, carried_send, carried_recv, carried_sem).wait_recv()

            def source(j):
                fade = carried_recv[step - 1][j, 2:4, :]
                return carried_recv[step - 1][j, 0:2, :] * fade, fade

            send_carried(step, source)

        if step + 1 < steps:
            forward()
        total = lax.fori_loop(0, nblocks // group, some, total)
        if step + 1 == steps:
            whole(step - 1, carried_send, carried_recv, carried_sem).wait_recv()
        masses = carried_recv[step - 1][:, 0:2, :]
        fade = carried_recv[step - 1][:, 2:4, :]
        left = masses * fade
        dep[...] = masses - left
        if step + 1 == steps:
            mass_out[...] = left
            total = all_deposits(step, total)
        if step + 1 == steps:
            for t in range(archs):
                q = BEDC // LANES
                bed_part[t] = (total[t * q : (t + 1) * q] + total[8 + t * q : 8 + (t + 1) * q]) * scale
            bed_copy = pltpu.make_async_remote_copy(
                src_ref=bed_part.at[twin], dst_ref=bed_recv, send_sem=bed_sem.at[0], recv_sem=bed_sem.at[1],
                device_id={"arch": twin}, device_id_type=MESH,
            )
            bed_copy.start()
        whole(step - 1, pos_send, pos_recv, pos_sem).wait_recv()
        if step + 1 < steps:
            send_places(step, lambda j, step=step: pos_recv[step - 1][j] + delta[j])

    last = steps - 2
    def finish(j, _):
        pos_out[:, pl.ds(pl.multiple_of(j * width, width), width)] = pos_recv[last][j] + delta[j]
        return 0

    lax.fori_loop(0, nblocks, finish, 0, unroll=16)
    bed_copy.wait_recv()
    bed_out[...] = bed_part[arch] + bed_recv[...]

    table_copy.wait_send()
    bed_copy.wait_send()
    for step in range(steps - 1):
        whole(step, carried_send, carried_recv, carried_sem).wait_send()
        whole(step, pos_send, pos_recv, pos_sem).wait_send()


def write_out(*refs):
    count = len(refs) // 2
    sem = refs[-1]
    copies = [pltpu.make_async_copy(refs[i], refs[count + i], sem.at[i]) for i in range(count)]
    for copy in copies:
        copy.start()
    for copy in copies:
        copy.wait()


def body(
    position, particle_mass, settling, walk_noise, velocity, diffusivity, block_tile, cell_index, bed_cell, route_code
):
    doms = lax.axis_size("dom")
    archs = lax.axis_size("arch")
    particles = position.shape[1]
    nblocks = block_tile.shape[2]
    width = particles // nblocks
    steps = cell_index.shape[0]
    slabs, _, _, cells = velocity.shape
    rows = cells // LANES
    half = width // LANES
    moves = steps - 1
    in_hbm = pl.BlockSpec(memory_space=pltpu.HBM)
    in_vmem = pl.BlockSpec(memory_space=pltpu.VMEM)
    vmem = pltpu.VMEM
    args = (
        position,
        particle_mass.reshape(nblocks, half, LANES),
        settling.reshape(nblocks, half, LANES),
        walk_noise,
        velocity.transpose(1, 2, 0, 3).reshape(3, slabs, cells),
        diffusivity.transpose(1, 0, 2).reshape(slabs, cells),
        block_tile,
        cell_index,
        bed_cell,
        route_code,
    )
    results = pl.pallas_call(
        functools.partial(
            kernel, doms, archs, nblocks, width, steps, slabs, rows, BEDC / particles
        ),
        out_shape=(
            pltpu.VMEM((3, particles), F32),
            pltpu.VMEM((nblocks, half, LANES), F32),
            pltpu.VMEM((BEDC // LANES, LANES), F32),
        ),
        in_specs=[in_hbm] * len(args),
        out_specs=(in_vmem, in_vmem, in_vmem),
        scratch_shapes=[
            vmem(args[0].shape, F32),
            vmem(args[1].shape, F32),
            vmem(args[2].shape, F32),
            vmem(args[3].shape, F32),
            vmem(args[4].shape, BF16),
            vmem(args[5].shape, BF16),
            pltpu.SMEM(args[6].shape, jnp.int32),
            vmem(args[7].shape, jnp.int32),
            vmem(args[8].shape, jnp.int32),
            pltpu.SMEM(args[9].shape, jnp.int32),
            vmem((4, slabs * rows, LANES), F32),
            vmem((archs, slabs, 4, rows, LANES), BF16),
            pltpu.SMEM((moves, nblocks), jnp.int32),
            vmem((nblocks, half, LANES), F32),
            vmem((nblocks, half, LANES), F32),
            vmem((nblocks, 3, width), F32),
            [vmem((nblocks, 2 * half, LANES), F32)] * moves,
            [vmem((nblocks, 2 * half, LANES), F32)] * moves,
            [vmem((nblocks, 3, width), F32)] * moves,
            [vmem((nblocks, 3, width), F32)] * moves,
            vmem((archs, BEDC // LANES, LANES), F32),
            vmem((BEDC // LANES, LANES), F32),
            pltpu.SemaphoreType.DMA((len(args),)),
            pltpu.SemaphoreType.DMA((2,)),
            pltpu.SemaphoreType.DMA((moves, 2)),
            pltpu.SemaphoreType.DMA((moves, 2)),
            pltpu.SemaphoreType.DMA((2,)),
        ],
        compiler_params=pltpu.CompilerParams(
            collective_id=0, has_side_effects=True, vmem_limit_bytes=60 * 1024 * 1024
        ),
    )(*args)
    places, masses, beds = pl.pallas_call(
        write_out,
        out_shape=tuple(jax.ShapeDtypeStruct(r.shape, F32) for r in results),
        in_specs=[in_vmem] * 3,
        out_specs=(in_hbm,) * 3,
        scratch_shapes=[pltpu.SemaphoreType.DMA((3,))],
    )(*(pltpu.with_memory_space_constraint(r, pltpu.VMEM) for r in results))
    return places, masses.reshape(particles), beds.reshape(1, BEDC)


def solution(mesh):
    return jax.shard_map(
        body,
        mesh=mesh,
        in_specs=(
            P(None, ("arch", "dom")),
            P(("arch", "dom")),
            P(("arch", "dom")),
            P(None, None, ("arch", "dom")),
            P(None, None, ("arch", "dom"), None),
            P(None, ("arch", "dom"), None),
            P(None, ("arch", "dom"), None),
            P(None, ("arch", "dom")),
            P(None, ("arch", "dom")),
            P(None, ("arch", "dom"), None),
        ),
        out_specs=(P(None, ("arch", "dom")), P(("arch", "dom")), P(("arch", "dom"), None)),
        check_vma=False,
    )
```

profile of v0, /device:TPU:0, one launch (start us, length us, event | category | flops | bytes accessed | tf_op | source)
XLA Modules:
  0.0 19.3 jit_solution(3998493754179465732)
XLA Ops:
  0.6 18.0 %shard_map.121 = (f32[3,4096]{1,0:T(4,128)S(1)}, f32[16,2,128]{2,1,0:T(2,128)S(1)}, f32[4,128]{1,0:T(4,128)S(1)}) custom-call(f32[3,4096]{1,0:T(4,128)} %pos_hbm.1, f32[16,2,128]{2,1,0:T(2,128)} %bitcast.11, f32[16,2,128]{2,1,0:T(2,128)} %bitcast.12, f32[3,3,4096]{2,1,0:T(4,128)} %noise_hbm.1, bf16[3,4,2048]{2,1,0:T(4,128)(2,1)} %bitcast.10, ...), custom_call_target="tpu_custom_call" | custom-call | tf_op jit(solution)/shard_map/pallas_call | solution.py:323
  18.7 0.7 %shard_map.122 = (f32[3,4096]{1,0:T(4,128)}, f32[16,2,128]{2,1,0:T(2,128)}, f32[4,128]{1,0:T(4,128)}) custom-call(f32[3,4096]{1,0:T(4,128)S(1)} %get-tuple-element.9.refs_0_, f32[16,2,128]{2,1,0:T(2,128)S(1)} %get-tuple-element.10.refs_1_, f32[4,128]{1,0:T(4,128)S(1)} %get-tuple-element.11.refs_2_), custom_call_target="tpu_custom_call" | custom-call | tf_op jit(solution)/shard_map/pallas_call | solution.py:367
where the time goes:
time: 19.5 us; the launch traced here: 19.3 us
  Pallas kernels  18.7 us (96%)
  between operations  0.64 us (3%)
    pallas_call x1, Pallas kernels, body(): pl.pallas_call(functools.partial(kernel, doms, archs, nblocks, width, ste...  18 us
    pallas_call x1, Pallas kernels, body(): pl.pallas_call(write_out, out_shape=tuple((jax.ShapeDtypeStruct(r.shape,...  0.66 us

commit v1 on v0

--- a/solution.py
+++ b/solution.py
@@ -149,7 +149,7 @@
             weights.append(jnp.concatenate([high, low], axis=0))
             hits.append(low_hits(cells))
         return lax.dot_general(
-            jnp.concatenate(weights, axis=1), jnp.concatenate(hits, axis=1),
+            jnp.concatenate(hits, axis=1), jnp.concatenate(weights, axis=1),
             (((1,), (1,)), ((), ())), preferred_element_type=F32,
         )
 
@@ -189,7 +189,7 @@
 
     third = (lax.broadcasted_iota(jnp.int32, (3, width), 0) == 2)
 
-    total = jnp.zeros((16, LANES), F32)
+    total = jnp.zeros((LANES, 16), F32)
 
     for copy in staged[7:]:
         copy.wait()
@@ -254,6 +254,7 @@
             mass_out[...] = left
             total = all_deposits(step, total)
         if step + 1 == steps:
+            total = total.T
             for t in range(archs):
                 q = BEDC // LANES
                 bed_part[t] = (total[t * q : (t + 1) * q] + total[8 + t * q : 8 + (t + 1) * q]) * scale

time: 19.5 us -> 19.5 us (level)
  no operation moved by 1% of the time
where the time goes in v1:
time: 19.5 us; the launch traced here: 19.4 us
  Pallas kernels  18.7 us (96%)
  between operations  0.64 us (3%)
    pallas_call x1, Pallas kernels, body(): pl.pallas_call(functools.partial(kernel, doms, archs, nblocks, width, ste...  18.1 us
    pallas_call x1, Pallas kernels, body(): pl.pallas_call(write_out, out_shape=tuple((jax.ShapeDtypeStruct(r.shape,...  0.66 us

profile of v1, /device:TPU:0, one launch (start us, length us, event | category | flops | bytes accessed | tf_op | source)
XLA Modules:
  0.0 19.4 jit_solution(10948432165138715042)
XLA Ops:
  0.6 18.1 %shard_map.121 = (f32[3,4096]{1,0:T(4,128)S(1)}, f32[16,2,128]{2,1,0:T(2,128)S(1)}, f32[4,128]{1,0:T(4,128)S(1)}) custom-call(f32[3,4096]{1,0:T(4,128)} %pos_hbm.1, f32[16,2,128]{2,1,0:T(2,128)} %bitcast.11, f32[16,2,128]{2,1,0:T(2,128)} %bitcast.12, f32[3,3,4096]{2,1,0:T(4,128)} %noise_hbm.1, bf16[3,4,2048]{2,1,0:T(4,128)(2,1)} %bitcast.10, ...), custom_call_target="tpu_custom_call" | custom-call | tf_op jit(solution)/shard_map/pallas_call | solution.py:324
  18.7 0.7 %shard_map.122 = (f32[3,4096]{1,0:T(4,128)}, f32[16,2,128]{2,1,0:T(2,128)}, f32[4,128]{1,0:T(4,128)}) custom-call(f32[3,4096]{1,0:T(4,128)S(1)} %get-tuple-element.9.refs_0_, f32[16,2,128]{2,1,0:T(2,128)S(1)} %get-tuple-element.10.refs_1_, f32[4,128]{1,0:T(4,128)S(1)} %get-tuple-element.11.refs_2_), custom_call_target="tpu_custom_call" | custom-call | tf_op jit(solution)/shard_map/pallas_call | solution.py:368

commit v2 on v1

--- a/solution.py
+++ b/solution.py
@@ -159,32 +159,26 @@
 
         return lax.fori_loop(0, nblocks // group, some, total)
 
-    channel_ids = lax.broadcasted_iota(jnp.int32, (16, 2 * 4 * rows), 1) // rows % 4
-    out_ids = lax.broadcasted_iota(jnp.int32, (16, 2 * 4 * rows), 0)
-    mix = jnp.where(
-        out_ids < 8,
-        jnp.where(channel_ids == out_ids, 0.5 * time_step, 0.0),
-        jnp.where(channel_ids == 3, time_step, 0.0),
-    ).astype(BF16)
+    place_rows = lax.broadcasted_iota(jnp.int32, (3, width), 0)
 
     def walk(step, blocks):
-        picked = []
+        moves = []
         for j in blocks:
             cells = cell[step : step + 1, pl.ds(pl.multiple_of(j * width, width), width)]
-            row_hit = jnp.where(high_bits(cells) == cell_rows, 1.0, 0.0).astype(BF16)
+            row_hit = high_bits(cells) == cell_rows
             local = lax.div(tile[step, 0, j], doms)
             both = jnp.concatenate(
                 [table[local, slab].reshape(4 * rows, LANES) for slab in (step, step + 1)], axis=0
             )
-            found = jnp.dot(both, low_hits(cells), preferred_element_type=F32).astype(BF16)
-            found = found.reshape(8, rows, width) * row_hit[None]
-            picked.append(found.reshape(8 * rows, width))
-        mixed = jnp.dot(mix, jnp.concatenate(picked, axis=1), preferred_element_type=F32)
-        moves = []
-        for i, j in enumerate(blocks):
-            part = mixed[:, i * width : (i + 1) * width]
+            found = jnp.dot(both, low_hits(cells), preferred_element_type=F32)
+            found = found.reshape(2, 4, rows, width)
+            sums = [
+                jnp.sum(jnp.where(row_hit, found[0, ch] + found[1, ch], 0.0), axis=0, keepdims=True)
+                for ch in range(4)
+            ]
+            drift = jnp.where(place_rows == 0, sums[0], jnp.where(place_rows == 1, sums[1], sums[2]))
             draw = noise[step, :, pl.ds(pl.multiple_of(j * width, width), width)]
-            moves.append(part[0:3] + jnp.sqrt(part[8:11]) * draw)
+            moves.append(0.5 * time_step * drift + jnp.sqrt(time_step * sums[3]) * draw)
         return moves
 
     third = (lax.broadcasted_iota(jnp.int32, (3, width), 0) == 2)

time: 19.5 us -> 19.5 us (level)
  no operation moved by 1% of the time
where the time goes in v2:
time: 19.5 us; the launch traced here: 19.4 us
  Pallas kernels  18.7 us (96%)
  between operations  0.64 us (3%)
    pallas_call x1, Pallas kernels, body(): pl.pallas_call(functools.partial(kernel, doms, archs, nblocks, width, ste...  18.1 us
    pallas_call x1, Pallas kernels, body(): pl.pallas_call(write_out, out_shape=tuple((jax.ShapeDtypeStruct(r.shape,...  0.66 us

profile of v2, /device:TPU:0, one launch (start us, length us, event | category | flops | bytes accessed | tf_op | source)
XLA Modules:
  0.0 19.4 jit_solution(15979738855260864261)
XLA Ops:
  0.6 18.1 %shard_map.121 = (f32[3,4096]{1,0:T(4,128)S(1)}, f32[16,2,128]{2,1,0:T(2,128)S(1)}, f32[4,128]{1,0:T(4,128)S(1)}) custom-call(f32[3,4096]{1,0:T(4,128)} %pos_hbm.1, f32[16,2,128]{2,1,0:T(2,128)} %bitcast.11, f32[16,2,128]{2,1,0:T(2,128)} %bitcast.12, f32[3,3,4096]{2,1,0:T(4,128)} %noise_hbm.1, bf16[3,4,2048]{2,1,0:T(4,128)(2,1)} %bitcast.10, ...), custom_call_target="tpu_custom_call" | custom-call | tf_op jit(solution)/shard_map/pallas_call | solution.py:318
  18.7 0.7 %shard_map.122 = (f32[3,4096]{1,0:T(4,128)}, f32[16,2,128]{2,1,0:T(2,128)}, f32[4,128]{1,0:T(4,128)}) custom-call(f32[3,4096]{1,0:T(4,128)S(1)} %get-tuple-element.9.refs_0_, f32[16,2,128]{2,1,0:T(2,128)S(1)} %get-tuple-element.10.refs_1_, f32[4,128]{1,0:T(4,128)S(1)} %get-tuple-element.11.refs_2_), custom_call_target="tpu_custom_call" | custom-call | tf_op jit(solution)/shard_map/pallas_call | solution.py:362

commit v3 on v2

--- a/solution.py
+++ b/solution.py
@@ -88,7 +88,7 @@
         copy.wait()
     fade = jnp.exp(-time_step * settle[...])
     decay[...] = fade
-    dep[...] = mass[...] * (1.0 - fade)
+    dep[0][...] = mass[...] * (1.0 - fade)
     mass[...] = mass[...] * fade
     find_inverse(0)
 
@@ -142,7 +142,7 @@
             cells = bed[step : step + 1, pl.ds(pl.multiple_of(j * width, width), width)]
             local = lax.div(tile[step, 0, j], doms)
             home = local * (BEDC // LANES) + high_bits(cells)
-            amount = jnp.concatenate([dep[j, 0:1, :], dep[j, 1:2, :]], axis=1)
+            amount = jnp.concatenate([dep[step][j, 0:1, :], dep[step][j, 1:2, :]], axis=1)
             weight = jnp.where(home == home_rows, amount, 0.0)
             high = weight.astype(BF16)
             low = (weight - high.astype(F32)).astype(BF16)
@@ -221,7 +221,8 @@
         def some(k, total, step=step):
             blocks = [k * group + i for i in range(group)]
             moves = walk(step, blocks)
-            total = total + deposits(step - 1, blocks)
+            if step + 1 == steps:
+                total = total + sum(deposits(earlier, blocks) for earlier in range(step))
             for j, move in zip(blocks, moves):
                 delta[j] = move
             return total
@@ -243,7 +244,7 @@
         masses = carried_recv[step - 1][:, 0:2, :]
         fade = carried_recv[step - 1][:, 2:4, :]
         left = masses * fade
-        dep[...] = masses - left
+        dep[step][...] = masses - left
         if step + 1 == steps:
             mass_out[...] = left
             total = all_deposits(step, total)
@@ -341,7 +342,7 @@
             vmem((archs, slabs, 4, rows, LANES), BF16),
             pltpu.SMEM((moves, nblocks), jnp.int32),
             vmem((nblocks, half, LANES), F32),
-            vmem((nblocks, half, LANES), F32),
+            [vmem((nblocks, half, LANES), F32)] * steps,
             vmem((nblocks, 3, width), F32),
             [vmem((nblocks, 2 * half, LANES), F32)] * moves,
             [vmem((nblocks, 2 * half, LANES), F32)] * moves,

time: 19.5 us -> 19.5 us (level)
  no operation moved by 1% of the time
where the time goes in v3:
time: 19.5 us; the launch traced here: 19.4 us
  Pallas kernels  18.7 us (96%)
  between operations  0.64 us (3%)
    pallas_call x1, Pallas kernels, body(): pl.pallas_call(functools.partial(kernel, doms, archs, nblocks, width, ste...  18.1 us
    pallas_call x1, Pallas kernels, body(): pl.pallas_call(write_out, out_shape=tuple((jax.ShapeDtypeStruct(r.shape,...  0.66 us

profile of v3, /device:TPU:0, one launch (start us, length us, event | category | flops | bytes accessed | tf_op | source)
XLA Modules:
  0.0 19.4 jit_solution(17250323260619947021)
XLA Ops:
  0.6 18.1 %shard_map.121 = (f32[3,4096]{1,0:T(4,128)S(1)}, f32[16,2,128]{2,1,0:T(2,128)S(1)}, f32[4,128]{1,0:T(4,128)S(1)}) custom-call(f32[3,4096]{1,0:T(4,128)} %pos_hbm.1, f32[16,2,128]{2,1,0:T(2,128)} %bitcast.11, f32[16,2,128]{2,1,0:T(2,128)} %bitcast.12, f32[3,3,4096]{2,1,0:T(4,128)} %noise_hbm.1, bf16[3,4,2048]{2,1,0:T(4,128)(2,1)} %bitcast.10, ...), custom_call_target="tpu_custom_call" | custom-call | tf_op jit(solution)/shard_map/pallas_call | solution.py:319
  18.7 0.7 %shard_map.122 = (f32[3,4096]{1,0:T(4,128)}, f32[16,2,128]{2,1,0:T(2,128)}, f32[4,128]{1,0:T(4,128)}) custom-call(f32[3,4096]{1,0:T(4,128)S(1)} %get-tuple-element.9.refs_0_, f32[16,2,128]{2,1,0:T(2,128)S(1)} %get-tuple-element.10.refs_1_, f32[4,128]{1,0:T(4,128)S(1)} %get-tuple-element.11.refs_2_), custom_call_target="tpu_custom_call" | custom-call | tf_op jit(solution)/shard_map/pallas_call | solution.py:363
